TPU v7x, 32 devices: a whole 2x2x4 slice. The times are simulated.
32 devices in a mesh: dp: 8 (over z, y), section: 4 (over x, core).
Axes of the slice: x: 2, y: 2, z: 4, core: 2. Of those that a mesh axis runs over, the one named last changes fastest.
Arguments:
- tokens: bfloat16 [16, 1024, 768], P('dp', 'section'), may hold values from -6 to 6
- seg_counts: int32 [16, 8], P('dp'), may hold values from 0 to 128, as said below
- w_in: bfloat16 [4, 768, 3072], P('section'), may hold values from -2 to 2
- w_down: bfloat16 [6144, 768], P('section'), may hold values from -0.109375 to 0.109375
- ln_gain: bfloat16 [4, 768], P('section'), may hold values from 0.5 to 1.5
- ln_bias: bfloat16 [4, 768], P('section'), may hold values from -1 to 1
- pos_table: bfloat16 [8, 768], P(None, 'section'), may hold values from -3 to 3
- cotangent: bfloat16 [16, 1024, 768], P('dp', 'section'), may hold values from -24 to 24
Outputs:
- mixed: bfloat16 [16, 1024, 768], P('dp', 'section')
- grad_tokens: float32 [16, 1024, 768], P('dp', 'section')
- grad_w_in: float32 [4, 768, 3072], P('section')
- grad_w_down: float32 [6144, 768], P('section')
- grad_gain: float32 [4, 768], P('section')
- grad_bias: float32 [4, 768], P('section')
- grad_pos: float32 [8, 768], P(None, 'section')
Inputs may be any that keep to these rules, and one draw needn't show every extreme that they name: `seg_counts`: segment j of a document holds min(128, max(0, length - j * 128)) tokens for the document's length, which is 128 or more; of the 2 documents of one dp index, one has all 1024 tokens and another at most (7) * 128.
All inputs are finite; a program needn't handle non-finite values.
Results may differ from a plain program's by a relative error of at most 0.02.
Values may be sent and summed in bfloat16 or wider, within the bound.
A program may use at most 192 MiB of HBM per device.

v0:
```python
from functools import partial

import jax
import jax.numpy as jnp
from jax import lax
from jax.sharding import PartitionSpec as P

D = 768
H = 12
FF = 3072
SEG = 128
SEGS = 8


epsilon = 1e-05
masked_score = -1e30


def from_behind(block, axis, distance):
    devices = range(lax.axis_size(axis))
    route = [(i - distance, i) for i in devices if i - distance in devices]
    return lax.ppermute(block, axis, route)


def for_sending(x):

    def short(part):
        return part.astype(jnp.bfloat16) if part.dtype == jnp.float32 else part

    return jax.tree.map(short, x)


def layer_norm(residual, gain_vector, bias_vector):
    mean_value = jnp.mean(residual, axis=-1, keepdims=True)
    center = residual - mean_value
    variance = jnp.mean(center * center, axis=-1, keepdims=True)
    return center * lax.rsqrt(variance + epsilon) * gain_vector + bias_vector


def split_heads(qkv, model_width, head_count):
    block_count, row_count = (qkv.shape[0], qkv.shape[1])
    head_size = model_width // head_count
    queries = qkv[..., :model_width].reshape(block_count, row_count, head_count, head_size)
    key_rows = qkv[..., model_width : 2 * model_width].reshape(
        block_count, row_count, head_count, head_size
    )
    values = qkv[..., 2 * model_width :].reshape(block_count, row_count, head_count, head_size)
    return (queries, key_rows, values)


def attend(rows, weight, visible, head_count):
    block_count, row_count, model_width = rows.shape
    head_size = model_width // head_count
    qkv = jnp.einsum(
        "nsd,de->nse", rows, weight[:, : 3 * model_width], preferred_element_type=jnp.float32
    ).astype(jnp.bfloat16)
    queries, key_rows, values = split_heads(qkv, model_width, head_count)
    scores = jnp.einsum(
        "nqhd,nkhd->nhqk", queries, key_rows, preferred_element_type=jnp.float32
    ) * head_size ** (-0.5)
    scores = jnp.where(visible[:, None, None, :], scores, masked_score)
    probability = jax.nn.softmax(scores, axis=-1)
    low_probability = probability.astype(jnp.bfloat16)
    context = jnp.einsum(
        "nhqk,nkhd->nqhd", low_probability, values, preferred_element_type=jnp.float32
    )
    context = context.astype(jnp.bfloat16).reshape(block_count, row_count, model_width)
    output = jnp.einsum(
        "nsc,rc->nsr", context, weight[:, 3 * model_width :], preferred_element_type=jnp.float32
    )
    return (output, (qkv, probability, low_probability, context))


def attend_back(rows, weight, head_count, grad_output, stored):
    qkv, probability, low_probability, context = stored
    block_count, row_count, model_width = rows.shape
    head_size = model_width // head_count
    queries, key_rows, values = split_heads(qkv, model_width, head_count)
    grad_context = jnp.einsum(
        "nsr,rc->nsc", grad_output, weight[:, 3 * model_width :], preferred_element_type=jnp.float32
    ).astype(jnp.bfloat16)
    grad_out_weight = jnp.einsum(
        "nsr,nsc->rc", grad_output, context, preferred_element_type=jnp.float32
    )
    grad_heads = grad_context.reshape(block_count, row_count, head_count, head_size)
    grad_prob = jnp.einsum(
        "nqhd,nkhd->nhqk", grad_heads, values, preferred_element_type=jnp.float32
    )
    grad_values = jnp.einsum(
        "nhqk,nqhd->nkhd", low_probability, grad_heads, preferred_element_type=jnp.float32
    ).astype(jnp.bfloat16)
    grad_scores = probability * (
        grad_prob - jnp.sum(grad_prob * probability, axis=-1, keepdims=True)
    )
    grad_scores = grad_scores.astype(jnp.bfloat16)
    grad_queries = (
        jnp.einsum("nhqk,nkhd->nqhd", grad_scores, key_rows, preferred_element_type=jnp.float32)
        * head_size ** (-0.5)
    ).astype(jnp.bfloat16)
    grad_keys = (
        jnp.einsum("nhqk,nqhd->nkhd", grad_scores, queries, preferred_element_type=jnp.float32)
        * head_size ** (-0.5)
    ).astype(jnp.bfloat16)
    flat_shape = (block_count, row_count, model_width)
    grad_qkv = jnp.concatenate(
        [
            grad_queries.reshape(flat_shape),
            grad_keys.reshape(flat_shape),
            grad_values.reshape(flat_shape),
        ],
        axis=-1,
    )
    grad_in_weight = jnp.einsum("nsd,nse->de", rows, grad_qkv, preferred_element_type=jnp.float32)
    grad_rows = jnp.einsum(
        "nse,de->nsd", grad_qkv, weight[:, : 3 * model_width], preferred_element_type=jnp.float32
    )
    return (grad_rows, jnp.concatenate([grad_in_weight, grad_out_weight], axis=1))


def feed_forward(rows, weight, down):
    pre_act = jnp.dot(rows, weight, preferred_element_type=jnp.float32)
    hidden = jax.nn.gelu(pre_act, approximate=False).astype(jnp.bfloat16)
    return (jnp.dot(hidden, down, preferred_element_type=jnp.float32), (pre_act, hidden))


def feed_back(rows, weight, down, grad_output, stored):
    pre_act, hidden = stored
    grad_hidden = jnp.einsum("rd,fd->rf", grad_output, down, preferred_element_type=jnp.float32)
    gelu_value, gelu_pull = jax.vjp(partial(jax.nn.gelu, approximate=False), pre_act)
    grad_pre = gelu_pull(grad_hidden)[0].astype(jnp.bfloat16)
    grad_weight = jnp.einsum("rd,rf->df", rows, grad_pre, preferred_element_type=jnp.float32)
    grad_down = jnp.einsum("rf,rd->fd", hidden, grad_output, preferred_element_type=jnp.float32)
    grad_rows = jnp.einsum("rf,df->rd", grad_pre, weight, preferred_element_type=jnp.float32)
    return (grad_rows, grad_weight, grad_down)


def shards(tokens, seg_counts, w_in, w_down, ln_gain, ln_bias, pos_table, cotangent):
    rows_all, pos_full, cot_all = (
        lax.all_gather(tokens, "section", axis=1, tiled=True),
        lax.all_gather(pos_table, "section", axis=1, tiled=True),
        lax.all_gather(cotangent, "section", axis=1, tiled=True),
    )
    lower_half = from_behind(w_down, "section", 1)
    down_full = jnp.concatenate([lower_half, w_down], axis=0)
    section_index = lax.axis_index("section")
    sections = lax.axis_size("section")
    weight = w_in[0]
    gain_vector = ln_gain[0].astype(jnp.float32)
    bias_vector = ln_bias[0].astype(jnp.float32)
    pos_wide = pos_full.astype(jnp.float32)
    batches = tokens.shape[0]
    length = SEGS * SEG
    position = jnp.arange(SEG, dtype=jnp.int32)[None, :]
    zeros_down = jnp.zeros((FF, D), jnp.float32)
    zeros_pos = jnp.zeros((SEGS, D), jnp.float32)
    zeros_rows = jnp.zeros((length, D), jnp.float32)
    zeros_low = jnp.zeros((length, D), jnp.bfloat16)
    bf_zero = jnp.zeros((), jnp.bfloat16)

    def norm_back(residual, grad_rows):
        normed, norm_pull = jax.vjp(layer_norm, residual, gain_vector, bias_vector)
        return norm_pull(grad_rows)

    def seg_attention(buffer, counts):
        blocks = buffer.reshape(SEGS, SEG, D)
        visible = position < jnp.maximum(counts, 1)[:, None]
        attended, stored = attend(blocks, weight, visible, H)
        return (blocks, blocks.astype(jnp.float32) + attended, stored)

    def forward_seg_attention(buffer, counts):
        blocks, residual, stored = seg_attention(buffer, counts)
        return (
            layer_norm(residual, gain_vector, bias_vector).astype(jnp.bfloat16).reshape(length, D)
        )

    def backward_seg_attention(buffer, grad_in, counts):
        blocks, residual, stored = seg_attention(buffer, counts)
        grad_res, grad_gain, grad_bias = norm_back(
            residual, grad_in.astype(jnp.float32).reshape(SEGS, SEG, D)
        )
        grad_rows, grad_weight = attend_back(
            blocks, weight, H, grad_res.astype(jnp.bfloat16), stored
        )
        grad_tokens = (grad_res + grad_rows).reshape(length, D)
        return (zeros_low, grad_weight, zeros_down, grad_gain, grad_bias, zeros_pos, grad_tokens)

    def mlp_rows(rows):
        output, stored = feed_forward(rows, weight, down_full)
        return (rows.astype(jnp.float32) + output, stored)

    def forward_seg_mlp(buffer, counts):
        residual, stored = mlp_rows(buffer)
        return layer_norm(residual, gain_vector, bias_vector).astype(jnp.bfloat16)

    def backward_seg_mlp(buffer, grad_in, counts):
        residual, stored = mlp_rows(buffer)
        grad_res, grad_gain, grad_bias = norm_back(residual, grad_in.astype(jnp.float32))
        grad_rows, grad_weight, grad_down = feed_back(
            buffer, weight, down_full, grad_res.astype(jnp.bfloat16), stored
        )
        grad_buffer = (grad_res + grad_rows).astype(jnp.bfloat16)
        return (grad_buffer, grad_weight, grad_down, grad_gain, grad_bias, zeros_pos, zeros_rows)

    def cross_attention(buffer, counts):
        blocks = buffer.reshape(SEGS, SEG, D)
        summary = (blocks[:, 0, :].astype(jnp.float32) + pos_wide).astype(jnp.bfloat16)
        attended, stored = attend(summary[None], weight, (counts > 0)[None], H)
        return (blocks, summary, summary.astype(jnp.float32) + attended[0], stored)

    def forward_cross_attention(buffer, counts):
        blocks, summary, residual, stored = cross_attention(buffer, counts)
        fresh = layer_norm(residual, gain_vector, bias_vector).astype(jnp.bfloat16)
        return blocks.at[:, 0, :].set(fresh).reshape(length, D)

    def backward_cross_attention(buffer, grad_in, counts):
        blocks, summary, residual, stored = cross_attention(buffer, counts)
        grad_blocks = grad_in.reshape(SEGS, SEG, D)
        grad_res, grad_gain, grad_bias = norm_back(
            residual, grad_blocks[:, 0, :].astype(jnp.float32)
        )
        grad_rows, grad_weight = attend_back(
            summary[None], weight, H, grad_res[None].astype(jnp.bfloat16), stored
        )
        grad_summary = (grad_res + grad_rows[0]).astype(jnp.bfloat16)
        grad_buffer = grad_blocks.at[:, 0, :].set(grad_summary).reshape(length, D)
        return (
            grad_buffer,
            grad_weight,
            zeros_down,
            grad_gain,
            grad_bias,
            grad_summary.astype(jnp.float32),
            zeros_rows,
        )

    def cross_mlp(buffer):
        blocks = buffer.reshape(SEGS, SEG, D)
        residual, stored = mlp_rows(blocks[:, 0, :])
        return (blocks, residual, stored)

    def forward_cross_mlp(buffer, counts):
        blocks, residual, stored = cross_mlp(buffer)
        fresh = layer_norm(residual, gain_vector, bias_vector).astype(jnp.bfloat16)
        live_rows = position < counts[:, None]
        joined = jnp.where(live_rows[:, :, None], blocks.at[:, 0, :].set(fresh), bf_zero)
        return joined.reshape(length, D)

    def backward_cross_mlp(buffer, grad_in, counts):
        blocks, residual, stored = cross_mlp(buffer)
        live_rows = position < counts[:, None]
        grad_blocks = jnp.where(live_rows[:, :, None], grad_in.reshape(SEGS, SEG, D), bf_zero)
        grad_res, grad_gain, grad_bias = norm_back(
            residual, grad_blocks[:, 0, :].astype(jnp.float32)
        )
        grad_rows, grad_weight, grad_down = feed_back(
            blocks[:, 0, :], weight, down_full, grad_res.astype(jnp.bfloat16), stored
        )
        grad_summary = (grad_res + grad_rows).astype(jnp.bfloat16)
        grad_buffer = grad_blocks.at[:, 0, :].set(grad_summary).reshape(length, D)
        return (grad_buffer, grad_weight, grad_down, grad_gain, grad_bias, zeros_pos, zeros_rows)

    forward_parts = [
        forward_seg_attention,
        forward_seg_mlp,
        forward_cross_attention,
        forward_cross_mlp,
    ]
    backward_parts = [
        backward_seg_attention,
        backward_seg_mlp,
        backward_cross_attention,
        backward_cross_mlp,
    ]

    def forward_tick(tick_index, state_tuple):
        incoming, kept, finals = state_tuple
        micro_batch = tick_index - section_index
        active = (micro_batch >= 0) & (micro_batch < batches)
        slot_index = jnp.clip(micro_batch, 0, batches - 1)
        own_rows = lax.dynamic_index_in_dim(rows_all, slot_index, 0, keepdims=False)
        section_in = jnp.where(section_index == 0, own_rows, incoming)
        counts = lax.dynamic_index_in_dim(seg_counts, slot_index, 0, keepdims=False)
        result = lax.switch(section_index, forward_parts, section_in, counts)
        old_kept = lax.dynamic_index_in_dim(kept, slot_index, 0, keepdims=False)
        kept = lax.dynamic_update_index_in_dim(
            kept, jnp.where(active, section_in, old_kept), slot_index, 0
        )
        old_final = lax.dynamic_index_in_dim(finals, slot_index, 0, keepdims=False)
        finals = lax.dynamic_update_index_in_dim(
            finals, jnp.where(active, result, old_final), slot_index, 0
        )
        incoming = jax.tree.map(
            lambda part, own: part.astype(own.dtype),
            from_behind(for_sending(result), "section", 1),
            result,
        )
        return (incoming, kept, finals)

    empty_batches = jnp.zeros((batches, length, D), jnp.bfloat16)
    incoming, kept, finals = lax.fori_loop(
        0, batches + sections - 1, forward_tick, (zeros_low, empty_batches, empty_batches)
    )
    final_terms = jnp.where(section_index == sections - 1, finals.astype(jnp.float32), 0.0)
    mixed = lax.psum_scatter(
        final_terms.astype(jnp.bfloat16), "section", scatter_dimension=1, tiled=True
    )

    def backward_tick(tick_index, state_tuple):
        incoming, totals, grad_all = state_tuple
        micro_batch = tick_index - (sections - 1 - section_index)
        active = (micro_batch >= 0) & (micro_batch < batches)
        slot_index = jnp.clip(micro_batch, 0, batches - 1)
        own_grad = lax.dynamic_index_in_dim(cot_all, slot_index, 0, keepdims=False)
        grad_in = jnp.where(section_index == sections - 1, own_grad, incoming)
        section_in = lax.dynamic_index_in_dim(kept, slot_index, 0, keepdims=False)
        counts = lax.dynamic_index_in_dim(seg_counts, slot_index, 0, keepdims=False)
        result = lax.switch(section_index, backward_parts, section_in, grad_in, counts)

        def add_active(total, term):
            return total + jnp.where(active, term, 0.0)

        totals = jax.tree.map(add_active, totals, tuple(result[1:6]))
        old_grad = lax.dynamic_index_in_dim(grad_all, slot_index, 0, keepdims=False)
        grad_all = lax.dynamic_update_index_in_dim(
            grad_all, jnp.where(active, result[6], old_grad), slot_index, 0
        )
        incoming = from_behind(for_sending(result[0]), "section", -1)
        return (incoming, totals, grad_all)

    zero_totals = (
        jnp.zeros((D, FF), jnp.float32),
        zeros_down,
        jnp.zeros((D,), jnp.float32),
        jnp.zeros((D,), jnp.float32),
        zeros_pos,
    )
    incoming, totals, grad_all = lax.fori_loop(
        0,
        batches + sections - 1,
        backward_tick,
        (zeros_low, zero_totals, jnp.zeros((batches, length, D), jnp.float32)),
    )
    grad_weight, grad_down, grad_gain, grad_bias, grad_pos_full = totals
    grad_tokens, pos_part = (
        lax.psum_scatter(
            grad_all.astype(jnp.bfloat16), "section", scatter_dimension=1, tiled=True
        ).astype(jnp.float32),
        lax.psum_scatter(
            grad_pos_full.astype(jnp.bfloat16), "section", scatter_dimension=1, tiled=True
        ).astype(jnp.float32),
    )
    half_rows = FF // 2
    weight_total, down_whole, gain_total, bias_total, pos_total = lax.psum(
        (grad_weight, grad_down, grad_gain, grad_bias, pos_part), "dp"
    )
    handed = from_behind(down_whole[:half_rows].astype(jnp.bfloat16), "section", -1).astype(
        jnp.float32
    )
    down_total = jnp.where(section_index % 2 == 0, handed, down_whole[half_rows:])
    return (
        mixed,
        grad_tokens,
        weight_total[None],
        down_total,
        gain_total[None],
        bias_total[None],
        pos_total,
    )


def solution(mesh):
    return jax.shard_map(
        shards,
        mesh=mesh,
        in_specs=(
            P("dp", "section", None),
            P("dp", None),
            P("section", None, None),
            P("section", None),
            P("section", None),
            P("section", None),
            P(None, "section"),
            P("dp", "section", None),
        ),
        out_specs=(
            P("dp", "section", None),
            P("dp", "section", None),
            P("section", None, None),
            P("section", None),
            P("section", None),
            P("section", None),
            P(None, "section"),
        ),
        check_vma=False,
    )
```

profile of v0, /device:TPU:0, one launch (start us, length us, event | category | flops | bytes accessed | tf_op | source)
XLA Modules:
  0.0 1868.9 jit_solution(13041912757934200522)
XLA Ops:
  23.7 22.0 %all-gather.4.cloned.1.call-done = bf16[2,1024,768]{2,1,0:T(8,128)(2,1)} async-done(((bf16[2,256,768]{2,1,0:T(8,128)(2,1)}), bf16[2,1024,768]{2,1,0:T(8,128)(2,1)}) %all-gather.4.cloned.1.call-update) | async-done | bytes 3145744 | tf_op jit(solution)/shard_map/all_gather | solution.py:139
  50.6 348.6 %while.53 = (s32[]{:T(128)}, bf16[1024,768]{1,0:T(8,128)(2,1)}, bf16[2,1024,768]{2,1,0:T(8,128)(2,1)}, bf16[2,1024,768]{2,1,0:T(8,128)(2,1)}, pred[]{:T(512)}, /...) while((s32[]{:T(128)}, bf16[1024,768]{1,0:T(8,128)(2,1)}, ...), condition=%wide.region_17.18_spmd.clone.clone, body=%wide.region_0.17_spmd.clone.clone.sunk | while | flops 9879159808 | bytes 125974776 | solution.py:300
  56.0 30.4 %conditional.8 = (bf16[1024,768]{1,0:T(8,128)(2,1)S(1)}) conditional(s32[]{:T(128)} %get-tuple-element.1606, (bf16[1024,768]{1,0:T(8,128)(2,1)S(1)}, bf16[768,3072]{1,0:T(8,128)(2,1)}, s32[1,128]{1,0:T(1,128)S(1)}, s32[8]{0:T(128)S(1)}, f32[768]{0:T(1024)S(1)}, /*index=5*/f32[768]{0:T(1024)S(1)}) %tuple.204, ...), branch_computations={%region_1.5_spmd, %region_6.8_spmd, %region_9.13_spmd, %region_14.... | conditional | flops 9876800512 | bytes 69350024 | solution.py:283
  86.4 31.6 %collective-permute-start = (bf16[1024,768]{1,0:T(8,128)(2,1)S(1)}, bf16[1024,768]{1,0:T(8,128)(2,1)S(1)}, u32[]{:S(2)}, u32[]{:S(2)}) collective-permute-start(bf16[1024,768]{1,0:T(8,128)(2,1)S(1)} %get-tuple-element.1682), channel_id=1, source_target_pairs={{0,1},{1,2},{2,3},{4,5},{5,6},{6,7},{8,9},{9,10},{10,11},{12,13},{... | collective-permute-start | bytes 4718600 | tf_op jit(solution)/shard_map/while/body/eval_jaxpr/ppermute | solution.py:22
  128.6 30.1 %conditional.8 = (bf16[1024,768]{1,0:T(8,128)(2,1)S(1)}) conditional(s32[]{:T(128)} %get-tuple-element.1606, (bf16[1024,768]{1,0:T(8,128)(2,1)S(1)}, bf16[768,3072]{1,0:T(8,128)(2,1)}, s32[1,128]{1,0:T(1,128)S(1)}, s32[8]{0:T(128)S(1)}, f32[768]{0:T(1024)S(1)}, /*index=5*/f32[768]{0:T(1024)S(1)}) %tuple.204, ...), branch_computations={%region_1.5_spmd, %region_6.8_spmd, %region_9.13_spmd, %region_14.... | conditional | flops 9876800512 | bytes 69350024 | solution.py:283
  158.7 28.4 %collective-permute-start = (bf16[1024,768]{1,0:T(8,128)(2,1)S(1)}, bf16[1024,768]{1,0:T(8,128)(2,1)S(1)}, u32[]{:S(2)}, u32[]{:S(2)}) collective-permute-start(bf16[1024,768]{1,0:T(8,128)(2,1)S(1)} %get-tuple-element.1682), channel_id=1, source_target_pairs={{0,1},{1,2},{2,3},{4,5},{5,6},{6,7},{8,9},{9,10},{10,11},{12,13},{... | collective-permute-start | bytes 4718600 | tf_op jit(solution)/shard_map/while/body/eval_jaxpr/ppermute | solution.py:22
  197.6 30.1 %conditional.8 = (bf16[1024,768]{1,0:T(8,128)(2,1)S(1)}) conditional(s32[]{:T(128)} %get-tuple-element.1606, (bf16[1024,768]{1,0:T(8,128)(2,1)S(1)}, bf16[768,3072]{1,0:T(8,128)(2,1)}, s32[1,128]{1,0:T(1,128)S(1)}, s32[8]{0:T(128)S(1)}, f32[768]{0:T(1024)S(1)}, /*index=5*/f32[768]{0:T(1024)S(1)}) %tuple.204, ...), branch_computations={%region_1.5_spmd, %region_6.8_spmd, %region_9.13_spmd, %region_14.... | conditional | flops 9876800512 | bytes 69350024 | solution.py:283
  227.7 28.4 %collective-permute-start = (bf16[1024,768]{1,0:T(8,128)(2,1)S(1)}, bf16[1024,768]{1,0:T(8,128)(2,1)S(1)}, u32[]{:S(2)}, u32[]{:S(2)}) collective-permute-start(bf16[1024,768]{1,0:T(8,128)(2,1)S(1)} %get-tuple-element.1682), channel_id=1, source_target_pairs={{0,1},{1,2},{2,3},{4,5},{5,6},{6,7},{8,9},{9,10},{10,11},{12,13},{... | collective-permute-start | bytes 4718600 | tf_op jit(solution)/shard_map/while/body/eval_jaxpr/ppermute | solution.py:22
  266.6 30.1 %conditional.8 = (bf16[1024,768]{1,0:T(8,128)(2,1)S(1)}) conditional(s32[]{:T(128)} %get-tuple-element.1606, (bf16[1024,768]{1,0:T(8,128)(2,1)S(1)}, bf16[768,3072]{1,0:T(8,128)(2,1)}, s32[1,128]{1,0:T(1,128)S(1)}, s32[8]{0:T(128)S(1)}, f32[768]{0:T(1024)S(1)}, /*index=5*/f32[768]{0:T(1024)S(1)}) %tuple.204, ...), branch_computations={%region_1.5_spmd, %region_6.8_spmd, %region_9.13_spmd, %region_14.... | conditional | flops 9876800512 | bytes 69350024 | solution.py:283
  296.7 28.4 %collective-permute-start = (bf16[1024,768]{1,0:T(8,128)(2,1)S(1)}, bf16[1024,768]{1,0:T(8,128)(2,1)S(1)}, u32[]{:S(2)}, u32[]{:S(2)}) collective-permute-start(bf16[1024,768]{1,0:T(8,128)(2,1)S(1)} %get-tuple-element.1682), channel_id=1, source_target_pairs={{0,1},{1,2},{2,3},{4,5},{5,6},{6,7},{8,9},{9,10},{10,11},{12,13},{... | collective-permute-start | bytes 4718600 | tf_op jit(solution)/shard_map/while/body/eval_jaxpr/ppermute | solution.py:22
  335.7 30.1 %conditional.8 = (bf16[1024,768]{1,0:T(8,128)(2,1)S(1)}) conditional(s32[]{:T(128)} %get-tuple-element.1606, (bf16[1024,768]{1,0:T(8,128)(2,1)S(1)}, bf16[768,3072]{1,0:T(8,128)(2,1)}, s32[1,128]{1,0:T(1,128)S(1)}, s32[8]{0:T(128)S(1)}, f32[768]{0:T(1024)S(1)}, /*index=5*/f32[768]{0:T(1024)S(1)}) %tuple.204, ...), branch_computations={%region_1.5_spmd, %region_6.8_spmd, %region_9.13_spmd, %region_14.... | conditional | flops 9876800512 | bytes 69350024 | solution.py:283
  365.8 28.4 %collective-permute-start = (bf16[1024,768]{1,0:T(8,128)(2,1)S(1)}, bf16[1024,768]{1,0:T(8,128)(2,1)S(1)}, u32[]{:S(2)}, u32[]{:S(2)}) collective-permute-start(bf16[1024,768]{1,0:T(8,128)(2,1)S(1)} %get-tuple-element.1682), channel_id=1, source_target_pairs={{0,1},{1,2},{2,3},{4,5},{5,6},{6,7},{8,9},{9,10},{10,11},{12,13},{... | collective-permute-start | bytes 4718600 | tf_op jit(solution)/shard_map/while/body/eval_jaxpr/ppermute | solution.py:22
  402.4 768.2 %while.54 = (s32[]{:T(128)}, bf16[1024,768]{1,0:T(8,128)(2,1)}, f32[768,3072]{0,1:T(8,128)}, f32[3072,768]{1,0:T(8,128)}, f32[768]{0:T(1024)}, /*index=5*/f32[76...) while((s32[]{:T(128)}, bf16[1024,768]{1,0:T(8,128)(2,1)}, ...), condition=%wide.region_54.55_spmd.clone.clone, body=%wide.region_19.54_spmd.clone.clone.sunk | while | flops 29294618624 | bytes 383228288 | solution.py:337
  413.8 121.5 %conditional.9 = (bf16[1024,768]{1,0:T(8,128)(2,1)}, f32[768,3072]{0,1:T(8,128)}, f32[3072,768]{1,0:T(8,128)}, f32[768]{0:T(1024)S(1)}, f32[768]{0:T(1024)}, /*i...) conditional(s32[]{:T(128)} %get-tuple-element.1669, ...), branch_computations={%region_20.29_spmd, %region_30.36_spmd, %region_37.46_spmd, %regio... | conditional | flops 29278867456 | bytes 285162496 | solution.py:317
  486.3 9.6 convolution_bitcast_fusion
  556.7 121.6 %conditional.9 = (bf16[1024,768]{1,0:T(8,128)(2,1)}, f32[768,3072]{0,1:T(8,128)}, f32[3072,768]{1,0:T(8,128)}, f32[768]{0:T(1024)S(1)}, f32[768]{0:T(1024)}, /*i...) conditional(s32[]{:T(128)} %get-tuple-element.1669, ...), branch_computations={%region_20.29_spmd, %region_30.36_spmd, %region_37.46_spmd, %regio... | conditional | flops 29278867456 | bytes 285162496 | solution.py:317
  629.2 9.7 convolution_bitcast_fusion
  707.1 121.6 %conditional.9 = (bf16[1024,768]{1,0:T(8,128)(2,1)}, f32[768,3072]{0,1:T(8,128)}, f32[3072,768]{1,0:T(8,128)}, f32[768]{0:T(1024)S(1)}, f32[768]{0:T(1024)}, /*i...) conditional(s32[]{:T(128)} %get-tuple-element.1669, ...), branch_computations={%region_20.29_spmd, %region_30.36_spmd, %region_37.46_spmd, %regio... | conditional | flops 29278867456 | bytes 285162496 | solution.py:317
  779.6 9.7 convolution_bitcast_fusion
  857.4 121.6 %conditional.9 = (bf16[1024,768]{1,0:T(8,128)(2,1)}, f32[768,3072]{0,1:T(8,128)}, f32[3072,768]{1,0:T(8,128)}, f32[768]{0:T(1024)S(1)}, f32[768]{0:T(1024)}, /*i...) conditional(s32[]{:T(128)} %get-tuple-element.1669, ...), branch_computations={%region_20.29_spmd, %region_30.36_spmd, %region_37.46_spmd, %regio... | conditional | flops 29278867456 | bytes 285162496 | solution.py:317
  930.0 9.7 convolution_bitcast_fusion
  983.7 11.3 select_add_fusion.9
  998.1 11.2 select_add_fusion.10
  1014.6 121.6 %conditional.9 = (bf16[1024,768]{1,0:T(8,128)(2,1)}, f32[768,3072]{0,1:T(8,128)}, f32[3072,768]{1,0:T(8,128)}, f32[768]{0:T(1024)S(1)}, f32[768]{0:T(1024)}, /*i...) conditional(s32[]{:T(128)} %get-tuple-element.1669, ...), branch_computations={%region_20.29_spmd, %region_30.36_spmd, %region_37.46_spmd, %regio... | conditional | flops 29278867456 | bytes 285162496 | solution.py:317
  1087.1 9.7 convolution_bitcast_fusion
  1140.8 11.3 select_add_fusion.9
  1155.1 11.2 select_add_fusion.10
  1170.6 9.6 copy.218
  1184.7 564.7 %all-reduce.4.cloned.1.call-done = (f32[1,768,3072]{2,1,0:T(8,128)}, f32[3072,768]{1,0:T(8,128)}) async-done(((f32[1,768,3072]{2,1,0:T(8,128)}, f32[3072,768]{1,0:T(8,128)}), (f32[1,768,3072]{2,1,0:T(8,128)}, f32[3072,768]{1,0:T(8,128)})) %all-reduce.4.cloned.1.call-update) | async-done | bytes 18874384 | tf_op jit(solution)/shard_map/psum | solution.py:353
  1753.3 18.2 reduce-scatter.10.cloned.1.call-done
  1772.3 37.7 %all-reduce = (f32[1,768]{1,0:T(1,128)}, f32[1,768]{1,0:T(1,128)}, f32[8,192]{1,0:T(8,128)}) all-reduce(f32[1,768]{1,0:T(1,128)S(1)} %broadcast_in_dim.268, f32[1,768]{1,0:T(1,128)S(1)} %broadcast_in_dim.269, bf16[8,192]{1,0:T(8,128)(2,1)S(1)} %copy.235), channel_id=1, replica_groups=mesh['dp'=8,'section'=4] {'dp'}, use_global_device_ids=true, to_apply=%region_58.59 | all-reduce | flops 3072 | bytes 21504 | tf_op jit(solution)/shard_map/psum | solution.py:353
  1820.0 33.0 %reduce-scatter.6.cloned.1.call-done = bf16[2,256,768]{2,1,0:T(8,128)(2,1)} async-done(((bf16[2,1024,768]{2,1,0:T(8,128)(2,1)}), bf16[2,256,768]{2,1,0:T(8,128)(2,1)}) %reduce-scatter.6.cloned.1.call-update) | async-done | bytes 786448 | tf_op jit(solution)/shard_map/reduce_scatter | solution.py:304
  (653 shorter events, 832.1 us)
Async XLA Ops:
  7.2 15.0 copy-start.23
  7.2 38.5 %all-gather.4.cloned.1.call-start = ((), (), s32[]{:S(2)}) async-start(), calls=%async_computation.3 | async-start | bytes 3932160 | tf_op jit(solution)/shard_map/all_gather | solution.py:139
  7.9 391.4 %all-gather.6.cloned.1.call-start = ((), (), s32[]{:S(2)}) async-start(), calls=%async_computation.5 | async-start | bytes 3932160 | tf_op jit(solution)/shard_map/all_gather | solution.py:141
  8.0 10.7 collective-permute-start.2
  11.7 1737.6 %all-reduce.4.cloned.1.call-start = ((), (), s32[]{:S(2)}) async-start(), calls=%async_computation.8 | async-start | bytes 37748736 | tf_op jit(solution)/shard_map/psum | solution.py:353
  86.4 34.6 %collective-permute-start = (bf16[1024,768]{1,0:T(8,128)(2,1)S(1)}, bf16[1024,768]{1,0:T(8,128)(2,1)S(1)}, u32[]{:S(2)}, u32[]{:S(2)}) collective-permute-start(bf16[1024,768]{1,0:T(8,128)(2,1)S(1)} %get-tuple-element.1682), channel_id=1, source_target_pairs={{0,1},{1,2},{2,3},{4,5},{5,6},{6,7},{8,9},{9,10},{10,11},{12,13},{... | collective-permute-start | bytes 4718600 | tf_op jit(solution)/shard_map/while/body/eval_jaxpr/ppermute | solution.py:22
  158.7 31.3 %collective-permute-start = (bf16[1024,768]{1,0:T(8,128)(2,1)S(1)}, bf16[1024,768]{1,0:T(8,128)(2,1)S(1)}, u32[]{:S(2)}, u32[]{:S(2)}) collective-permute-start(bf16[1024,768]{1,0:T(8,128)(2,1)S(1)} %get-tuple-element.1682), channel_id=1, source_target_pairs={{0,1},{1,2},{2,3},{4,5},{5,6},{6,7},{8,9},{9,10},{10,11},{12,13},{... | collective-permute-start | bytes 4718600 | tf_op jit(solution)/shard_map/while/body/eval_jaxpr/ppermute | solution.py:22
  227.7 31.4 %collective-permute-start = (bf16[1024,768]{1,0:T(8,128)(2,1)S(1)}, bf16[1024,768]{1,0:T(8,128)(2,1)S(1)}, u32[]{:S(2)}, u32[]{:S(2)}) collective-permute-start(bf16[1024,768]{1,0:T(8,128)(2,1)S(1)} %get-tuple-element.1682), channel_id=1, source_target_pairs={{0,1},{1,2},{2,3},{4,5},{5,6},{6,7},{8,9},{9,10},{10,11},{12,13},{... | collective-permute-start | bytes 4718600 | tf_op jit(solution)/shard_map/while/body/eval_jaxpr/ppermute | solution.py:22
  296.7 31.4 %collective-permute-start = (bf16[1024,768]{1,0:T(8,128)(2,1)S(1)}, bf16[1024,768]{1,0:T(8,128)(2,1)S(1)}, u32[]{:S(2)}, u32[]{:S(2)}) collective-permute-start(bf16[1024,768]{1,0:T(8,128)(2,1)S(1)} %get-tuple-element.1682), channel_id=1, source_target_pairs={{0,1},{1,2},{2,3},{4,5},{5,6},{6,7},{8,9},{9,10},{10,11},{12,13},{... | collective-permute-start | bytes 4718600 | tf_op jit(solution)/shard_map/while/body/eval_jaxpr/ppermute | solution.py:22
  365.8 31.4 %collective-permute-start = (bf16[1024,768]{1,0:T(8,128)(2,1)S(1)}, bf16[1024,768]{1,0:T(8,128)(2,1)S(1)}, u32[]{:S(2)}, u32[]{:S(2)}) collective-permute-start(bf16[1024,768]{1,0:T(8,128)(2,1)S(1)} %get-tuple-element.1682), channel_id=1, source_target_pairs={{0,1},{1,2},{2,3},{4,5},{5,6},{6,7},{8,9},{9,10},{10,11},{12,13},{... | collective-permute-start | bytes 4718600 | tf_op jit(solution)/shard_map/while/body/eval_jaxpr/ppermute | solution.py:22
  536.5 14.9 collective-permute-start.1
  679.5 22.2 %collective-permute-start.1 = (bf16[1024,768]{1,0:T(8,128)(2,1)}, bf16[1024,768]{1,0:T(8,128)(2,1)S(1)}, u32[]{:S(2)}, u32[]{:S(2)}) collective-permute-start(bf16[1024,768]{1,0:T(8,128)(2,1)} %get-tuple-element.1522), channel_id=1, source_target_pairs={{1,0},{2,1},{3,2},{5,4},{6,5},{7,6},{9,8},{10,9},{11,10},{13,12},{... | collective-permute-start | bytes 4718600 | tf_op jit(solution)/shard_map/while/body/eval_jaxpr/ppermute | solution.py:22
  829.9 22.2 %collective-permute-start.1 = (bf16[1024,768]{1,0:T(8,128)(2,1)}, bf16[1024,768]{1,0:T(8,128)(2,1)S(1)}, u32[]{:S(2)}, u32[]{:S(2)}) collective-permute-start(bf16[1024,768]{1,0:T(8,128)(2,1)} %get-tuple-element.1522), channel_id=1, source_target_pairs={{1,0},{2,1},{3,2},{5,4},{6,5},{7,6},{9,8},{10,9},{11,10},{13,12},{... | collective-permute-start | bytes 4718600 | tf_op jit(solution)/shard_map/while/body/eval_jaxpr/ppermute | solution.py:22
  842.0 10.1 copy-start.25
  980.2 29.0 %collective-permute-start.1 = (bf16[1024,768]{1,0:T(8,128)(2,1)}, bf16[1024,768]{1,0:T(8,128)(2,1)S(1)}, u32[]{:S(2)}, u32[]{:S(2)}) collective-permute-start(bf16[1024,768]{1,0:T(8,128)(2,1)} %get-tuple-element.1522), channel_id=1, source_target_pairs={{1,0},{2,1},{3,2},{5,4},{6,5},{7,6},{9,8},{10,9},{11,10},{13,12},{... | collective-permute-start | bytes 4718600 | tf_op jit(solution)/shard_map/while/body/eval_jaxpr/ppermute | solution.py:22
  983.6 11.4 copy-start.22
  983.7 11.4 copy-start.24
  995.0 14.2 copy-start.25
  998.0 11.2 copy-start.29
  998.1 11.2 copy-start.32
  1137.4 29.0 %collective-permute-start.1 = (bf16[1024,768]{1,0:T(8,128)(2,1)}, bf16[1024,768]{1,0:T(8,128)(2,1)S(1)}, u32[]{:S(2)}, u32[]{:S(2)}) collective-permute-start(bf16[1024,768]{1,0:T(8,128)(2,1)} %get-tuple-element.1522), channel_id=1, source_target_pairs={{1,0},{2,1},{3,2},{5,4},{6,5},{7,6},{9,8},{10,9},{11,10},{13,12},{... | collective-permute-start | bytes 4718600 | tf_op jit(solution)/shard_map/while/body/eval_jaxpr/ppermute | solution.py:22
  1140.8 11.4 copy-start.22
  1140.8 11.4 copy-start.24
  1152.2 14.1 copy-start.25
  1155.1 11.2 copy-start.29
  1155.1 11.2 copy-start.32
  1180.2 591.2 %reduce-scatter.10.cloned.1.call-start = ((), (), s32[]{:S(2)}) async-start(), calls=%async_computation.7 | async-start | bytes 245760
  1181.8 630.1 %reduce-scatter.8.cloned.1.call-start = ((), (), s32[]{:S(2)}) async-start(), calls=%async_computation.6 | async-start | bytes 3932160 | tf_op jit(solution)/shard_map/reduce_scatter | solution.py:345
  1182.4 670.6 %reduce-scatter.6.cloned.1.call-start = ((), (), s32[]{:S(2)}) async-start(), calls=%async_computation.4 | async-start | bytes 3932160 | tf_op jit(solution)/shard_map/reduce_scatter | solution.py:304
  1184.7 568.6 %copy-start.30 = (f32[768]{0:T(1024)S(1)}, f32[768]{0:T(1024)}, u32[]{:S(2)}) copy-start(f32[768]{0:T(1024)} %get-tuple-element.897) | copy-start | bytes 9220
  1184.7 568.6 %copy-start.33 = (f32[768]{0:T(1024)S(1)}, f32[768]{0:T(1024)}, u32[]{:S(2)}) copy-start(f32[768]{0:T(1024)} %get-tuple-element.898) | copy-start | bytes 9220
  1751.9 62.3 %collective-permute-start.3 = (bf16[1536,768]{1,0:T(8,128)(2,1)S(1)}, bf16[1536,768]{1,0:T(8,128)(2,1)}, u32[]{:S(2)}, u32[]{:S(2)}) collective-permute-start(bf16[1536,768]{1,0:T(8,128)(2,1)S(1)} %slice.252), channel_id=1, source_target_pairs={{1,0},{2,1},{3,2},{5,4},{6,5},{7,6},{9,8},{10,9},{11,10},{13,12},{... | collective-permute-start | bytes 7077896 | tf_op jit(solution)/shard_map/ppermute | solution.py:22
  (127 other events, 526.4 us)
Sparse Core Ops, SparseCore 0:
  9.6 36.0 all-gather.3
  47.3 32.1 all-gather.5
  1180.4 568.9 all-reduce.3
  1752.2 19.2 reduce-scatter.9
  1773.9 37.9 reduce-scatter.7
  1815.0 37.9 reduce-scatter.5
where the time goes:
time: 1900 us; the launch traced here: 1870 us
  waiting for transfers between devices  641 us (34%)
  matrix products  422 us (22%)
  local copies, waits for them, and re-layouts  245 us (13%)
  other arithmetic  245 us (13%)
  starting transfers between devices  160 us (8%)
  loops' own time  98.4 us (5%)
  blocking collectives  43 us (2%)
    psum x1, waiting for transfers between devices, shards(): lax.psum((grad_weight, grad_down, grad_gain, grad_bias, pos_part), 'dp')  565 us
    ppermute x12, starting transfers between devices, from_behind(): return lax.ppermute(block, axis, route)  160 us
    add x20, other arithmetic, add_active(): return total + jnp.where(active, term, 0.0)  89.1 us
    another operation x5, loops' own time, backward_tick(): lax.switch(section_index, backward_parts, section_in, grad_in, counts)  85.5 us
    sub x10, matrix products, attend(): probability = jax.nn.softmax(scores, axis=-1)  73.1 us
    dot_general x10, matrix products, attend(): jnp.einsum('nsd,de->nse', rows, weight[:, :3 * model_width], preferred_el...  60.6 us
    dot_general x5, matrix products, attend_back(): jnp.einsum('nsd,nse->de', rows, grad_qkv, preferred_element_type=jnp.floa...  48.3 us
    slice x20, local copies, waits for them, and re-layouts, split_heads(): qkv[..., model_width:2 * model_width]  43.2 us
  transfers between devices with their start and end apart: 18, of which 5 were waited for; matrix products, arithmetic and copies ran while one was open for 17% of the time, Pallas kernels for 0%

commit v1 on v0

v1 whole, which is shorter than its diff:
```python
import functools

import jax
import jax.numpy as jnp
from jax import lax
from jax.experimental import pallas as pl
from jax.experimental.pallas import tpu as pltpu
from jax.sharding import PartitionSpec as P

bf16 = jnp.bfloat16
f32 = jnp.float32
D = 768
FF = 3072
ROWS = 1024
CH = 512
MESH = pl.DeviceIdType.MESH


class Refs:
    pass


def nn(a, b):
    return lax.dot_general(a, b, (((1,), (0,)), ((), ())), preferred_element_type=f32)


def nt(a, b):
    return lax.dot_general(a, b, (((1,), (1,)), ((), ())), preferred_element_type=f32)


def tn(a, b):
    return lax.dot_general(a, b, (((0,), (0,)), ((), ())), preferred_element_type=f32)


def cut(start, size):
    return pl.ds(pl.multiple_of(start, size), size)


def loop(n, body):
    def step(i, carry):
        body(i)
        return carry

    lax.fori_loop(0, n, step, 0)


def norm_stats(r):
    mean = jnp.mean(r, axis=-1, keepdims=True)
    cen = r - mean
    var = jnp.mean(cen * cen, axis=-1, keepdims=True)
    rstd = lax.rsqrt(var + 1e-5)
    return cen * rstd, rstd


def norm_back(dy, xhat, rstd, gain):
    dx = dy * gain
    m1 = jnp.mean(dx, axis=-1, keepdims=True)
    m2 = jnp.mean(dx * xhat, axis=-1, keepdims=True)
    return rstd * (dx - m1 - xhat * m2)


def gelu_parts(u):
    ax = jnp.abs(u)
    e = jnp.exp(u * u * -0.5)
    t = 1.0 / (1.0 + (0.3275911 * 0.7071067811865476) * ax)
    h = 0.7107068705 + t * (-0.7265760135 + t * 0.5307027145)
    h = t * (0.127414796 + t * (-0.142248368 + t * h)) * e
    phi = jnp.where(u >= 0, 1.0 - h, h)
    return u * phi, phi + u * (0.3989422804014327 * e)


def stacked(v):
    low = lax.broadcasted_iota(jnp.int32, v.shape, 1) < 64
    z = jnp.zeros_like(v)
    return jnp.concatenate([jnp.where(low, v, z), jnp.where(low, z, v)], axis=0)


def beside(v):
    low = lax.broadcasted_iota(jnp.int32, (128, 128), 1) < 64
    return jnp.where(low, v[:128], v[128:])


def attn_block(R, i, vis):
    rs = cut(i * 128, 128)
    for j in range(6):
        q2 = R.qkv[rs, 128 * j : 128 * j + 128]
        k2 = R.qkv[rs, 768 + 128 * j : 768 + 128 * j + 128]
        v2 = R.qkv[rs, 1536 + 128 * j : 1536 + 128 * j + 128]
        s = jnp.where(vis, nt(stacked(q2), k2) * 0.125, -1e30)
        s = jnp.exp(s - jnp.max(s, axis=-1, keepdims=True))
        pr = (s / jnp.sum(s, axis=-1, keepdims=True)).astype(bf16)
        R.p[cut(i * 1536 + 256 * j, 256), :] = pr
        R.ctx[rs, 128 * j : 128 * j + 128] = beside(nn(pr, v2)).astype(bf16)


def attn_block_back(R, i):
    rs = cut(i * 128, 128)
    for j in range(6):
        sq, sk, sv = [slice(b + 128 * j, b + 128 * j + 128) for b in (0, 768, 1536)]
        q2 = R.qkv[rs, sq]
        k2 = R.qkv[rs, sk]
        v2 = R.qkv[rs, sv]
        qs = stacked(q2)
        dos = stacked(R.xh1[rs, sq])
        pr = R.p[cut(i * 1536 + 256 * j, 256), :]
        pf = pr.astype(f32)
        dp = nt(dos, v2)
        ds = (pf * (dp - jnp.sum(dp * pf, axis=-1, keepdims=True))).astype(bf16)
        R.qkv[rs, sv] = tn(pr, dos).astype(bf16)
        R.qkv[rs, sq] = beside(nn(ds, k2) * 0.125).astype(bf16)
        R.qkv[rs, sk] = (tn(ds, qs) * 0.125).astype(bf16)


def qkv_half(R, r0):
    def body(n):
        cs = cut(n * 256, 256)
        R.qkv[pl.ds(r0, 512), cs] = nn(R.x[pl.ds(r0, 512), :], R.wall[0, :, cs]).astype(bf16)

    loop(9, body)


def attn_half(R, h):
    key = lax.broadcasted_iota(jnp.int32, (256, 128), 1)

    def seg(k):
        i = h * 4 + k
        attn_block(R, i, key < jnp.maximum(R.count_of(i), 1))

    loop(4, seg)


def attn_out(R, h):
    def body(k):
        rs = cut(h * 512 + k * 128, 128)
        att = nt(R.ctx[rs, :], R.wall[0, :, 2304:])
        xh, rstd = norm_stats(R.x[rs, :].astype(f32) + att)
        R.xh0[rs, :] = xh.astype(bf16)
        R.rs0[rs, :] = rstd
        R.a0[rs, :] = (xh * R.gains[0, 0:1, :] + R.gains[0, 1:2, :]).astype(bf16)

    loop(4, body)


def ffn_half(R, h):
    r0 = h * 512

    def up(n):
        cs = cut(n * 256, 256)
        mm, gg = gelu_parts(nn(R.a0[pl.ds(r0, 512), :], R.wall[1, :, cs]))
        R.m[pl.ds(r0, 512), cs] = mm.astype(bf16)
        R.gp[pl.ds(r0, 512), cs] = gg.astype(bf16)

    loop(12, up)

    def down(k):
        rs = cut(r0 + k * 256, 256)
        xh, rstd = norm_stats(R.a0[rs, :].astype(f32) + nn(R.m[rs, :], R.v0[...]))
        R.xh1[rs, :] = xh.astype(bf16)
        R.rs1[rs, :] = rstd
        R.a1[rs, :] = (xh * R.gains[1, 0:1, :] + R.gains[1, 1:2, :]).astype(bf16)

    loop(2, down)


def pad16(v):
    return jnp.concatenate([v, jnp.zeros_like(v)], axis=0).astype(bf16)


def first_ffn(R):
    rows = [R.a0[i * 128 : i * 128 + 16, :].astype(f32)[0:1, :] for i in range(8)]
    af = jnp.concatenate(rows, axis=0)
    a16 = pad16(af)

    def up(n):
        cs = cut(n * 256, 256)
        mm, gg = gelu_parts(nn(a16, R.wall[1, :, cs]))
        R.fm[:, cs] = mm.astype(bf16)
        R.fg[:, cs] = gg

    loop(12, up)
    xh, rstd = norm_stats(af + nn(R.fm[...], R.v0[...])[0:8])
    R.fxh[...] = xh
    R.frs[...] = rstd
    return (xh * R.gains[1, 0:1, :] + R.gains[1, 1:2, :]).astype(bf16).astype(f32)


def ln1_back(R):
    row = lax.broadcasted_iota(jnp.int32, (128, 1), 0)

    def body(i):
        rs = cut(i * 128, 128)
        live = (row < R.count_of(i)) & (row > 0)
        dy = jnp.where(live, R.cot[rs, :].astype(f32), 0.0)
        xh = R.xh1[rs, :].astype(f32)
        R.gsum[2:3, :] += jnp.sum(dy * xh, axis=0, keepdims=True)
        R.gsum[3:4, :] += jnp.sum(dy, axis=0, keepdims=True)
        dr = norm_back(dy, xh, R.rs1[rs, :], R.gains[1, 0:1, :])
        R.da0[rs, :] = dr
        R.cot[rs, :] = dr.astype(bf16)

    loop(8, body)


def row_pass(R):
    def hid(n):
        cs = cut(n * 256, 256)

        def part(k):
            rs = cut(k * 512, 512)
            dm = nt(R.cot[rs, :], R.v0[cs, :])
            R.gp[rs, cs] = (dm * R.gp[rs, cs].astype(f32)).astype(bf16)

        loop(2, part)

    loop(12, hid)

    def back(k):
        rs = cut(k * 256, 256)
        R.da0[rs, :] += nt(R.gp[rs, :], R.wall[1])

    loop(4, back)


def put_first(ref, i, rowval):
    rs = slice(i * 128, i * 128 + 16)
    blk = ref[rs, :]
    it = lax.broadcasted_iota(jnp.int32, blk.shape, 0)
    ref[rs, :] = jnp.where(it == 0, rowval.astype(f32), blk.astype(f32)).astype(blk.dtype)


def first_back(R, dc):
    xh = R.fxh[...]
    R.gsum[2:3, :] += jnp.sum(dc * xh, axis=0, keepdims=True)
    R.gsum[3:4, :] += jnp.sum(dc, axis=0, keepdims=True)
    dr = norm_back(dc, xh, R.frs[...], R.gains[1, 0:1, :])
    dz = pad16(dr)

    def hid(n):
        cs = cut(n * 256, 256)
        R.fdu[:, cs] = (nt(dz, R.v0[cs, :]) * R.fg[:, cs]).astype(bf16)

    loop(12, hid)
    da = dr + nt(R.fdu[...], R.wall[1])[0:8]
    for i in range(8):
        put_first(R.cot, i, dr[i : i + 1, :].astype(bf16))
        put_first(R.gp, i, R.fdu[...].astype(f32)[i : i + 1, :])
        put_first(R.da0, i, da[i : i + 1, :])


def transposes1(R):
    for b, ref in ((0, R.a0), (1536, R.cot)):

        def body(k, b=b, ref=ref):
            R.v0[b : b + 768, cut(k * 256, 256)] = ref[cut(k * 256, 256), :].T

        loop(3, body)
        R.v0[b + 768 : b + 1536, 0:256] = ref[768:1024, :].T


def tdot(R, b, rhs, cs):
    head = nn(R.v0[b : b + 768, :], rhs[0:768, cs])
    return head + nn(R.v0[b + 768 : b + 1536, 0:256], rhs[768:1024, cs])


def dvt_block(R, n):
    cs = cut(n * 256, 256)
    R.m[0:768, cs] = tdot(R, 1536, R.m, cs).astype(bf16)


def dw1_block(R, n):
    cs = cut(n * 256, 256)
    R.wall[1, :, cs] = tdot(R, 0, R.gp, cs).astype(bf16)


def ln0_back(R):
    def body(i):
        rs = cut(i * 128, 128)
        dy = R.da0[rs, :].astype(bf16).astype(f32)
        xh = R.xh0[rs, :].astype(f32)
        R.gsum[0:1, :] += jnp.sum(dy * xh, axis=0, keepdims=True)
        R.gsum[1:2, :] += jnp.sum(dy, axis=0, keepdims=True)
        dr = norm_back(dy, xh, R.rs0[rs, :], R.gains[0, 0:1, :])
        R.da0[rs, :] = dr
        R.a1[rs, :] = dr.astype(bf16)

    loop(8, body)


def dctx_pass(R):
    def body(k):
        rs = cut(k * 256, 256)
        R.xh1[rs, :] = nn(R.a1[rs, :], R.wall[0, :, 2304:]).astype(bf16)

    loop(4, body)


def transposes2(R):
    for c0, ref in ((0, R.x), (1024, R.a1)):

        def body(k, c0=c0, ref=ref):
            R.gp[0:768, cut(c0 + k * 256, 256)] = ref[cut(k * 256, 256), :].T

        loop(4, body)


def dx_pass(R):
    def body(k):
        rs = cut(k * 256, 256)
        R.cot[rs, :] = (R.da0[rs, :] + nt(R.qkv[rs, :], R.wall[0, :, :2304])).astype(bf16)

    loop(4, body)


def dw0_block(R, n):
    cs = pl.ds(n * 256, 256)
    if n < 9:
        R.wall[0, :, cs] = nn(R.gp[0:768, 0:1024], R.qkv[:, cs]).astype(bf16)
    else:
        c2 = pl.ds(n * 256 - 2304, 256)
        R.wall[0, :, cs] = nn(R.gp[0:768, 1024:2048], R.ctx[:, c2]).astype(bf16)


def cross_attn(R, pos_rows):
    g = R.gath[...].reshape(128, 896)
    cp = (g[:, :768] + jnp.concatenate([pos_rows] * 8, axis=0)).astype(bf16)
    R.x[0:128, :] = cp
    live = g[:, 768:896].T
    row = lax.broadcasted_iota(jnp.int32, (128, 128), 0)
    col = lax.broadcasted_iota(jnp.int32, (128, 128), 1)
    same = (row & 0x72) == (col & 0x72)
    vis = same & (live > 0.5)
    R.cmask[...] = jnp.where(vis, 1.0, 0.0)

    def qkv(n):
        cs = cut(n * 256, 256)
        R.qkv[0:128, cs] = nn(R.x[0:128, :], R.wall[1, :, cs]).astype(bf16)

    loop(9, qkv)
    mask = R.cmask[...] > 0.5
    attn_block(R, 0, jnp.concatenate([mask, mask], axis=0))
    att = nt(R.ctx[0:128, :], R.wall[1, :, 2304:])
    xh, rstd = norm_stats(R.x[0:128, :].astype(f32) + att)
    R.da0[0:128, :] = xh
    R.rs0[0:128, :] = rstd
    R.a0[0:128, :] = (xh * R.gains[0, 0:1, :] + R.gains[0, 1:2, :]).astype(bf16)


def cross_attn_back(R):
    dy = R.cot[0:128, :].astype(f32)
    xh = R.da0[0:128, :]
    R.gsum[0:1, :] = jnp.sum(dy * xh, axis=0, keepdims=True)
    R.gsum[1:2, :] = jnp.sum(dy, axis=0, keepdims=True)
    dr = norm_back(dy, xh, R.rs0[0:128, :], R.gains[0, 0:1, :])
    R.da0[0:128, :] = dr
    R.a1[0:128, :] = dr.astype(bf16)
    R.xh1[0:128, :] = nn(R.a1[0:128, :], R.wall[1, :, 2304:]).astype(bf16)
    attn_block_back(R, 0)
    dcp = R.da0[0:128, :] + nt(R.qkv[0:128, :], R.wall[1, :, :2304])
    R.da0[128:256, :] = dcp.astype(bf16).astype(f32)


def cross_attn_weights(R):
    R.gp[128:896, 0:128] = R.x[0:128, :].T
    R.gp[128:896, 128:256] = R.a1[0:128, :].T

    def one(n):
        cs = cut(n * 256, 256)
        R.wall[1, :, cs] = nn(R.gp[128:896, 0:128], R.qkv[0:128, cs]).astype(bf16)

    loop(9, one)

    def two(n):
        c2 = cut(n * 256, 256)
        cs = cut(2304 + n * 256, 256)
        R.wall[1, :, cs] = nn(R.gp[128:896, 128:256], R.ctx[0:128, c2]).astype(bf16)

    loop(3, two)


def cross_ffn(R):
    def up(n):
        cs = cut(n * 256, 256)
        mm, gg = gelu_parts(nn(R.a0[0:128, :], R.wall[0, :, cs]))
        R.gp[896:1024, cs] = mm.astype(bf16)
        R.gp[0:128, cs] = gg.astype(bf16)

    loop(12, up)
    xh, rstd = norm_stats(R.a0[0:128, :].astype(f32) + nn(R.gp[896:1024, :], R.v0[...]))
    R.da0[0:128, :] = xh
    R.rs0[0:128, :] = rstd
    R.da0[128:256, :] = xh * R.gains[0, 0:1, :] + R.gains[0, 1:2, :]


def cross_ffn_back(R):
    dy = R.gath[...].reshape(128, 896)[:, :768]
    xh = R.da0[0:128, :]
    R.gsum[0:1, :] = jnp.sum(dy * xh, axis=0, keepdims=True)
    R.gsum[1:2, :] = jnp.sum(dy, axis=0, keepdims=True)
    dr = norm_back(dy, xh, R.rs0[0:128, :], R.gains[0, 0:1, :])
    R.da0[0:128, :] = dr
    R.cot[0:128, :] = dr.astype(bf16)

    def hid(n):
        cs = cut(n * 256, 256)
        dm = nt(R.cot[0:128, :], R.v0[cs, :])
        R.gp[0:128, cs] = (dm * R.gp[0:128, cs].astype(f32)).astype(bf16)

    loop(12, hid)
    R.a1[0:128, :] = (R.da0[0:128, :] + nt(R.gp[0:128, :], R.wall[0])).astype(bf16)


def cross_ffn_weights(R):
    R.qkv[0:768, 0:128] = R.a0[0:128, :].T
    R.qkv[0:768, 128:256] = R.cot[0:128, :].T

    def body(n):
        cs = cut(n * 256, 256)
        R.wall[0, :, cs] = nn(R.qkv[0:768, 0:128], R.gp[0:128, cs]).astype(bf16)
        R.gp[128:896, cs] = nn(R.qkv[0:768, 128:256], R.gp[896:1024, cs]).astype(bf16)

    loop(12, body)


SCRATCH = dict(
    wall=((2, D, FF), bf16),
    v0=((FF, D), bf16),
    x=((ROWS, D), bf16),
    qkv=((ROWS, 2304), bf16),
    p=((12288, 128), bf16),
    ctx=((ROWS, D), bf16),
    xh0=((ROWS, D), bf16),
    rs0=((ROWS, 1), f32),
    a0=((ROWS, D), bf16),
    m=((ROWS, FF), bf16),
    gp=((ROWS, FF), bf16),
    xh1=((ROWS, D), bf16),
    rs1=((ROWS, 1), f32),
    a1=((ROWS, D), bf16),
    cot=((ROWS, D), bf16),
    da0=((ROWS, D), f32),
    gains=((2, 8, D), f32),
    gsum=((8, D), f32),
    gtot=((8, D), f32),
    gsr=((8, 8, D), f32),
    fm=((16, FF), bf16),
    fg=((16, FF), f32),
    fdu=((16, FF), bf16),
    fxh=((8, D), f32),
    frs=((8, 1), f32),
    cmask=((128, 128), f32),
    gath=((8, 16, 896), f32),
    cx=((8, 896), f32),
    cxr=((2, 8, 896), f32),
    ctmp=((4, 16, D), bf16),
    cfs=((8, D), f32),
    cfr=((4, 8, D), f32),
    dcs=((2, 8, D), f32),
    dcr=((8, D), f32),
    a3s=((16, D), f32),
    posf=((8, 192), f32),
    posr=((4, 8, 192), f32),
    gps=((4, 8, 192), f32),
    rx=((D, 4608), bf16),
    yb=((5, 384, CH), bf16),
    zb=((5, 3, 96, CH), bf16),
)
SEMS = dict(
    load=16, ctmp=4, ws=2, wr=2, vs=1, vr=1, gns=1, gnr=1, tks=2, tkr=2, pos_s=1, pos_r=4, cfs_s=1, cfr_r=4,
    cx_s=1, cx_r=2, gat_s=8, gat_r=8, a2_s=1, a2_r=1, a3_s=4, a3_r=1, da2_s=1, da2_r=1, dc_s=2, dc_r=1,
    gp_s=4, gp_r=1, dv_s=1, dv_r=1, a1_s=1, a1_r=1, a1_l=1, gt_s=1, gt_r=1, gt_l=1, gs_s=8, gs_r=8, og=1, ow=2,
    s1_s=9, s1_r=9, xf_s=9, xf_r=9, y_s=9, y_r=9, z_s=27, z_r=27, g_s=27, g_r=27, h_s=9, h_r=9, b_s=9, b_r=9, out=9,
)


def kernel(
    counts, tokens, cotan, w_in, w_down, gain, bias, pos,
    o_a1, o_a3, o_gt, o_g, o_gg, o_pos, *scratch,
):
    R, S = Refs(), Refs()
    for name, ref in zip(SCRATCH, scratch):
        setattr(R, name, ref)
    for name, ref in zip(SEMS, scratch[len(SCRATCH) :]):
        setattr(S, name, ref)

    dp = lax.axis_index("dp")
    sec = lax.axis_index("section")
    z, y = lax.div(dp, 2), lax.rem(dp, 2)
    xx, c = lax.div(sec, 2), lax.rem(sec, 2)

    def at(px, pc):
        return {"section": px * 2 + pc}

    def at_dp(pz, py):
        return {"dp": pz * 2 + py}

    core_peer, x_peer, diag = at(xx, 1 - c), at(1 - xx, c), at(1 - xx, 1 - c)
    y_peer = at_dp(z, 1 - y)
    z_peers = [at_dp(z ^ d, y) for d in (1, 2, 3)]
    dp_peers = [{"dp": dp ^ d} for d in range(1, 8)]

    def rcopy(src, dst, ss, rs, dev):
        return pltpu.make_async_remote_copy(
            src_ref=src, dst_ref=dst, send_sem=ss, recv_sem=rs, device_id=dev, device_id_type=MESH
        )

    def lcopy(src, dst, sem):
        return pltpu.make_async_copy(src, dst, sem)

    def count_of(i):
        return counts[lax.rem(lax.div(i, 2), 2), 2 * (c + 2 * lax.div(i, 4)) + lax.rem(i, 2)]

    R.count_of = count_of
    is0, is1 = xx == 0, xx == 1
    c0, c1 = c == 0, c == 1

    barrier = pltpu.get_barrier_semaphore()
    partners = [core_peer, x_peer, diag] + dp_peers
    for dev in partners:
        pl.semaphore_signal(barrier, inc=1, device_id=dev, device_id_type=MESH)

    own_w = lcopy(w_in, R.wall.at[jnp.where(is0, c, 1 - c)], S.load.at[0])
    own_v = lcopy(w_down, R.v0.at[cut(c * 1536, 1536)], S.load.at[1])
    own_x = lcopy(tokens, R.x.at[0:512], S.load.at[2])
    own_ct = lcopy(cotan, R.cot.at[0:512], S.load.at[3])
    heads = [lcopy(cotan.at[pl.ds(k * 128, 16)], R.ctmp.at[k], S.ctmp.at[k]) for k in range(4)]

    @pl.when(is0)
    def _():
        own_x.start()

    own_w.start()

    @pl.when(is0 | c1)
    def _():
        own_v.start()

    for cp in heads:
        cp.start()
    R.gsum[...] = jnp.zeros_like(R.gsum)
    gslot = jnp.where(is0, c, 0)
    R.gains[gslot, 0:1, :] = gain[...].astype(f32)
    R.gains[gslot, 1:2, :] = bias[...].astype(f32)
    R.posf[...] = pos[...].astype(f32)
    for cp in heads:
        cp.wait()
    first_rows = []
    for k in range(4):
        n = counts[k // 2, 2 * sec + k % 2]
        r = R.ctmp[k].astype(f32)[0:1, :]
        first_rows.append(jnp.where(n > 0, r, 0.0))
    R.cfs[...] = jnp.concatenate(first_rows + first_rows, axis=0)

    pl.semaphore_wait(barrier, len(partners))

    send_w = rcopy(w_in, R.wall.at[c], S.ws.at[0], S.wr.at[0], core_peer)
    send_v = rcopy(w_down, R.v0.at[cut(c * 1536, 1536)], S.vs.at[0], S.vr.at[0], core_peer)
    send_g = rcopy(R.gains.at[c], R.gains.at[c], S.gns.at[0], S.gnr.at[0], core_peer)
    send_x = rcopy(tokens, R.x.at[512:1024], S.tks.at[0], S.tkr.at[0], x_peer)
    send_ct = rcopy(cotan, R.cot.at[512:1024], S.tks.at[1], S.tkr.at[1], x_peer)
    other_w = rcopy(w_in, R.wall.at[1 - c], S.ws.at[0], S.wr.at[0], core_peer)
    other_v = rcopy(w_down, R.v0.at[cut((1 - c) * 1536, 1536)], S.vs.at[0], S.vr.at[0], core_peer)
    other_g = rcopy(R.gains.at[1 - c], R.gains.at[1 - c], S.gns.at[0], S.gnr.at[0], core_peer)

    def pos_copy(dev):
        return rcopy(R.posf, R.posr.at[sec], S.pos_s.at[0], S.pos_r.at[sec], dev)

    def cf_copy(dev):
        return rcopy(R.cfs, R.cfr.at[sec], S.cfs_s.at[0], S.cfr_r.at[sec], dev)

    def each_to(make, target):
        by = {2: (x_peer, diag, core_peer), 3: (diag, x_peer, core_peer)}[target]
        for s, dev in zip((0, 1, 5 - target), by):

            @pl.when(sec == s)
            def _(dev=dev):
                make(dev).start()

    def each_sent(make, target):
        @pl.when(sec != target)
        def _():
            make(core_peer).wait_send()

    @pl.when(is0)
    def _():
        send_w.start()
        send_g.start()
        send_v.start()

    @pl.when(is1)
    def _():
        send_x.start()

    each_to(pos_copy, 2)
    each_to(cf_copy, 3)

    def part_of(own, q):
        if q < 3:
            return R.m.at[0:768, pl.ds(pl.multiple_of(own * 1536 + q * CH, CH), CH)]
        return R.wall.at[own, :, pl.ds((q - 3) * CH, CH)]

    def add_rows(dst, r0, terms, n, step):
        def body(k):
            rs = pl.ds(pl.multiple_of(r0 + k * step, 32), step)
            total = dst[rs, :].astype(f32)
            for ref in terms:
                total = total + ref[pl.ds(pl.multiple_of(k * step, 32), step), :].astype(f32)
            dst[rs, :] = total.astype(bf16)

        loop(n // step, body)

    def s1_copy(q):
        return rcopy(
            part_of(1 - c, q), R.rx.at[:, pl.ds(q * CH, CH)], S.s1_s.at[q], S.s1_r.at[q], core_peer
        )

    def xf_copy(q):
        return rcopy(part_of(c, q), part_of(c, q), S.xf_s.at[q], S.xf_r.at[q], x_peer)

    def y_copy(q):
        half = part_of(c, q).at[pl.ds(pl.multiple_of((1 - y) * 384, 384), 384), :]
        return rcopy(half, R.yb.at[q // 2], S.y_s.at[q], S.y_r.at[q], y_peer)

    def z_copies(q):
        made = []
        for d in (1, 2, 3):
            piece = part_of(c, q).at[pl.ds(pl.multiple_of(y * 384 + (z ^ d) * 96, 96), 96), :]
            k = q * 3 + d - 1
            made.append(
                rcopy(piece, R.zb.at[q // 2, d - 1], S.z_s.at[k], S.z_r.at[k], z_peers[d - 1])
            )
        return made

    def g_copies(q):
        made = []
        piece = R.rx.at[pl.ds(pl.multiple_of(y * 384 + z * 96, 96), 96), pl.ds(q * CH, CH)]
        for d in (1, 2, 3):
            k = q * 3 + d - 1
            made.append(rcopy(piece, piece, S.g_s.at[k], S.g_r.at[k], z_peers[d - 1]))
        return made

    def h_copy(q):
        half = R.rx.at[pl.ds(pl.multiple_of(y * 384, 384), 384), pl.ds(q * CH, CH)]
        return rcopy(half, half, S.h_s.at[q], S.h_r.at[q], y_peer)

    def b_copy(q):
        cs = pl.ds(q * CH, CH)
        return rcopy(R.rx.at[:, cs], o_g.at[:, cs], S.b_s.at[q], S.b_r.at[q], x_peer)

    def out_copy(q):
        cs = pl.ds(q * CH, CH)
        return lcopy(R.rx.at[:, cs], o_g.at[:, cs], S.out.at[q])

    def chip_sum(q):
        s1_copy(q).wait_recv()
        add_rows(part_of(c, q), 0, [R.rx.at[:, pl.ds(q * CH, CH)]], 768, 64)
        if q % 2 == 0:
            y_copy(q).start()
        else:
            xf_copy(q).start()

    def step_a(q):
        xf_copy(q).wait_recv()
        y_copy(q).start()

    def step_b(q):
        y_copy(q).wait()
        mine = part_of(c, q)
        add_rows(mine, y * 384, [R.yb.at[q // 2]], 384, 64)
        for cp in z_copies(q):
            cp.start()

    def step_c(q):
        for cp in z_copies(q):
            cp.wait()
        r0 = pl.multiple_of(y * 384 + z * 96, 96)
        total = part_of(c, q)[pl.ds(r0, 96), :].astype(f32)
        for d in range(3):
            total = total + R.zb[q // 2, d].astype(f32)
        R.rx[pl.ds(r0, 96), pl.ds(q * CH, CH)] = total.astype(bf16)
        for cp in g_copies(q):
            cp.start()

    def step_d(q):
        for cp in g_copies(q):
            cp.wait()
        h_copy(q).start()

    def step_e0(q):
        h_copy(q).wait()
        out_copy(q).start()

    def step_e1(q):
        h_copy(q).wait()
        b_copy(q).start()

    def staged(qs, steps):
        for t in range(len(qs) + len(steps) - 1):
            for k, step in enumerate(steps):
                if 0 <= t - k < len(qs):
                    step(qs[t - k])

    def cx_copy(dev):
        return rcopy(R.cx, R.cxr.at[c], S.cx_s.at[0], S.cx_r.at[c], dev)

    def dc_copy(k, dev):
        return rcopy(R.dcs.at[k], R.dcr, S.dc_s.at[k], S.dc_r.at[0], dev)

    def a3_copy(k, dev):
        return rcopy(R.a3s, o_a3, S.a3_s.at[k], S.a3_r.at[0], dev)

    def gp_copy(s, dev):
        return rcopy(R.gps.at[s], o_pos, S.gp_s.at[s], S.gp_r.at[0], dev)

    a1_copy = rcopy(R.a1.at[512:1024], o_a1, S.a1_s.at[0], S.a1_r.at[0], x_peer)
    gt_copy = rcopy(R.cot.at[512:1024], o_gt, S.gt_s.at[0], S.gt_r.at[0], x_peer)
    a1_own = lcopy(R.a1.at[0:512], o_a1, S.a1_l.at[0])
    gt_own = lcopy(R.cot.at[0:512], o_gt, S.gt_l.at[0])
    gg_own = lcopy(R.gtot, o_gg, S.og.at[0])

    @pl.when(is0)
    def _():
        own_x.wait()
        own_ct.start()

        @pl.when(c0)
        def _():
            own_w.wait()

        @pl.when(c1)
        def _():
            other_w.wait_recv()

        other_g.wait_recv()
        qkv_half(R, 0)
        attn_half(R, 0)
        attn_out(R, 0)

        @pl.when(c1)
        def _():
            own_w.wait()

        @pl.when(c0)
        def _():
            other_w.wait_recv()

        own_v.wait()
        other_v.wait_recv()
        ffn_half(R, 0)
        send_x.wait_recv()
        qkv_half(R, 512)
        attn_half(R, 1)
        attn_out(R, 1)
        R.cx[:, 0:768] = first_ffn(R)
        it = lax.broadcasted_iota(jnp.int32, (8, 128), 0)
        flags = jnp.zeros((8, 128), f32)
        for i in range(8):
            flags = jnp.where((it == i) & (count_of(jnp.int32(i)) > 0), 1.0, flags)
        R.cx[:, 768:896] = flags

        @pl.when(c0)
        def _():
            cx_copy(x_peer).start()

        @pl.when(c1)
        def _():
            cx_copy(diag).start()

        ffn_half(R, 1)
        a1_copy.start()
        a1_own.start()
        own_ct.wait()
        send_ct.wait_recv()
        ln1_back(R)
        row_pass(R)
        dc_copy(0, core_peer).wait_recv()
        first_back(R, R.dcr[...])
        transposes1(R)
        for q in range(3):
            for n in (2 * q, 2 * q + 1, 6 + 2 * q, 7 + 2 * q):
                dvt_block(R, n)
            s1_copy(q).start()
            if q > 0:
                chip_sum(q - 1)
        for q in range(3, 9):
            dw1_block(R, 2 * (q - 3))
            dw1_block(R, 2 * (q - 3) + 1)

            @pl.when(c0)
            def _(q=q):
                s1_copy(q).start()

            if q == 3:
                chip_sum(2)
            else:

                @pl.when(c1)
                def _(q=q):
                    chip_sum(q - 1)

        a1_copy.wait_send()
        a1_own.wait()
        ln0_back(R)

        @pl.when(c1)
        def _():
            chip_sum(8)

        step_b(0)
        chip_g = rcopy(R.gsum, R.gsr.at[0], S.gs_s.at[0], S.gs_r.at[0], core_peer)
        chip_g.start()
        dctx_pass(R)
        chip_g.wait_recv()
        R.gtot[...] = R.gsum[...] + R.gsr[0]
        gsends = [
            rcopy(R.gtot, R.gsr.at[d], S.gs_s.at[d], S.gs_r.at[d], dp_peers[d - 1])
            for d in range(1, 8)
        ]
        for cp in gsends:
            cp.start()
        transposes2(R)
        step_c(0)

        def seg(i):
            attn_block_back(R, i)

            @pl.when(i == 1)
            def _():
                step_d(0)
                step_b(2)

            @pl.when(i == 3)
            def _():
                step_c(2)

                @pl.when(c1)
                def _():
                    step_b(4)

            @pl.when(i == 5)
            def _():
                step_e0(0)
                step_d(2)

                @pl.when(c1)
                def _():
                    step_c(4)
                    step_b(6)

            @pl.when(i == 7)
            def _():
                @pl.when(c1)
                def _():
                    step_d(4)
                    step_c(6)
                    step_b(8)

        loop(8, seg)
        dx_pass(R)
        gt_copy.start()
        gt_own.start()
        step_e0(2)

        @pl.when(c1)
        def _():
            step_e0(4)
            step_d(6)
            step_c(8)

        for k, q in enumerate(range(3, 9)):
            dw0_block(R, 2 * (q - 3))
            dw0_block(R, 2 * (q - 3) + 1)

            @pl.when(c1)
            def _(q=q):
                s1_copy(q).start()

            if q > 3:

                @pl.when(c0)
                def _(q=q):
                    chip_sum(q - 1)

        @pl.when(c0)
        def _():
            chip_sum(8)
            staged([4, 6, 8], [step_b, step_c, step_d, step_e0])

        @pl.when(c1)
        def _():
            step_e0(6)
            step_d(8)
            step_e0(8)

        for cp in gsends:
            cp.wait()
        total = R.gsum[...] + R.gsr[0]
        for d in range(1, 8):
            total = total + R.gsr[d]
        pair = jnp.where(c0, total[0:2], total[2:4])
        R.gtot[...] = jnp.concatenate([pair] * 4, axis=0)
        gg_own.start()
        send_w.wait_send()
        send_g.wait_send()
        send_v.wait_send()
        each_sent(pos_copy, 2)
        each_sent(cf_copy, 3)
        cx_copy(diag).wait_send()
        chip_g.wait_send()
        gt_copy.wait_send()
        gt_own.wait()
        for q in range(9):
            if q < 3:
                s1_copy(q).wait_send()
            else:

                @pl.when(c0)
                def _(q=q):
                    s1_copy(q).wait_send()

                @pl.when(c1)
                def _(q=q):
                    s1_copy(q).wait_send()

            if q % 2 == 1:
                xf_copy(q).wait_send()
                b_copy(q).wait_recv()
            else:
                out_copy(q).wait()
        a3_copy(0, diag).wait_recv()
        gp_copy(0, diag).wait_recv()
        gg_own.wait()

    def share(block):
        R.gath[dp] = block
        made = [
            rcopy(R.gath.at[dp], R.gath.at[dp], S.gat_s.at[d], S.gat_r.at[d], dp_peers[d - 1])
            for d in range(1, 8)
        ]
        for cp in made:
            cp.start()
        for d in range(1, 8):
            there = R.gath.at[dp ^ d]
            rcopy(there, there, S.gat_s.at[d], S.gat_r.at[d], dp_peers[d - 1]).wait_recv()
        return made

    @pl.when(is1)
    def _():
        send_x.wait_send()
        send_ct.start()

    @pl.when(is1 & c0)
    def _():
        rcopy(w_down, R.v0.at[0:1536], S.vs.at[0], S.vr.at[0], core_peer).start()
        for s in (0, 1, 3):
            rcopy(R.posf, R.posr.at[s], S.pos_s.at[0], S.pos_r.at[s], core_peer).wait_recv()
        R.posr[2] = R.posf[...]
        table = jnp.concatenate([R.posr[s] for s in range(4)], axis=1)
        picks = []
        for r in range(16):
            j = 2 * (r // 8 + 2 * ((r // 4) % 2)) + r % 2
            picks.append(table[j : j + 1, :])
        pos_rows = jnp.concatenate(picks, axis=0)
        for k in range(2):
            rcopy(R.cx, R.cxr.at[k], S.cx_s.at[0], S.cx_r.at[k], x_peer).wait_recv()
        own_w.wait()
        made = share(jnp.concatenate([R.cxr[0], R.cxr[1]], axis=0))
        cross_attn(R, pos_rows)
        a2 = rcopy(R.a0.at[0:128], R.a0.at[0:128], S.a2_s.at[0], S.a2_r.at[0], core_peer)
        a2.start()
        da2 = rcopy(R.a1.at[0:128], R.cot.at[0:128], S.da2_s.at[0], S.da2_r.at[0], core_peer)
        da2.wait_recv()
        cross_attn_back(R)
        for k in range(2):
            R.dcs[k] = R.da0[cut(128 + dp * 16 + k * 8, 8), :]
        dc_copy(0, x_peer).start()
        dc_copy(1, diag).start()
        rr = lax.broadcasted_iota(jnp.int32, (8, 128), 1)
        jj = lax.broadcasted_iota(jnp.int32, (8, 128), 0)
        seg_of = 2 * (((rr >> 3) & 1) + 2 * ((rr >> 2) & 1)) + (rr & 1)
        pick = jnp.where(seg_of == jj, 1.0, 0.0).astype(bf16)
        dpos = nn(pick, R.da0[128:256, :].astype(bf16))
        for s in range(4):
            R.gps[s] = dpos[:, 192 * s : 192 * s + 192]
        gp_copy(0, x_peer).start()
        gp_copy(1, diag).start()
        gp_copy(3, core_peer).start()
        gp_own = lcopy(R.gps.at[2], o_pos, S.gp_s.at[2])
        gp_own.start()
        R.gtot[...] = R.gsum[...]
        gg_own.start()
        cross_attn_weights(R)
        w_out = lcopy(R.wall.at[1], o_g.at[:, 1536:4608], S.ow.at[0])
        w_out.start()
        rcopy(w_down, R.v0.at[0:1536], S.vs.at[0], S.vr.at[0], core_peer).wait_send()
        each_sent(cf_copy, 3)
        for cp in made:
            cp.wait_send()
        a2.wait_send()
        dc_copy(0, x_peer).wait_send()
        dc_copy(1, diag).wait_send()
        gp_copy(0, x_peer).wait_send()
        gp_copy(1, diag).wait_send()
        gp_copy(3, core_peer).wait_send()
        gp_own.wait()
        gg_own.wait()
        w_out.wait()
        rcopy(R.a3s, o_a3, S.a3_s.at[0], S.a3_r.at[0], core_peer).wait_recv()

    @pl.when(is1 & c1)
    def _():
        for s in (0, 1, 2):
            rcopy(R.cfs, R.cfr.at[s], S.cfs_s.at[0], S.cfr_r.at[s], core_peer).wait_recv()
        R.cfr[3] = R.cfs[...]
        block = jnp.concatenate([R.cfr[k, 0:4] for k in (0, 2, 1, 3)], axis=0)
        made = share(jnp.concatenate([block, jnp.zeros((16, 128), f32)], axis=1))
        own_w.wait()
        own_v.wait()
        rcopy(w_down, R.v0.at[0:1536], S.vs.at[0], S.vr.at[0], core_peer).wait_recv()
        rcopy(R.a0.at[0:128], R.a0.at[0:128], S.a2_s.at[0], S.a2_r.at[0], core_peer).wait_recv()
        cross_ffn(R)
        R.a3s[...] = R.da0[cut(128 + dp * 16, 16), :]
        a3_copy(0, diag).start()
        a3_copy(1, x_peer).start()
        a3_copy(2, core_peer).start()
        a3_own = lcopy(R.a3s, o_a3, S.a3_s.at[3])
        a3_own.start()
        cross_ffn_back(R)
        da2 = rcopy(R.a1.at[0:128], R.cot.at[0:128], S.da2_s.at[0], S.da2_r.at[0], core_peer)
        da2.start()
        R.gtot[...] = R.gsum[...]
        gg_own.start()
        cross_ffn_weights(R)
        dv = rcopy(
            R.gp.at[128:896, 0:1536], o_g.at[:, 0:1536], S.dv_s.at[0], S.dv_r.at[0], core_peer
        )
        dv.start()
        w_out = lcopy(R.wall.at[0], o_g.at[:, 1536:4608], S.ow.at[0])
        v_out = lcopy(R.gp.at[128:896, 1536:3072], o_g.at[:, 0:1536], S.ow.at[1])
        w_out.start()
        v_out.start()
        each_sent(pos_copy, 2)
        for cp in made:
            cp.wait_send()
        a3_copy(0, diag).wait_send()
        a3_copy(1, x_peer).wait_send()
        a3_copy(2, core_peer).wait_send()
        a3_own.wait()
        da2.wait_send()
        gg_own.wait()
        dv.wait_send()
        w_out.wait()
        v_out.wait()
        gp_copy(0, core_peer).wait_recv()

    @pl.when(is1)
    def _():
        send_ct.wait_send()
        staged([1], [step_a, step_b, step_c, step_d, step_e1])
        staged([3, 5, 7], [step_a, step_b, step_c, step_d, step_e1])
        a1_copy.wait_recv()
        gt_copy.wait_recv()
        for q in (1, 3, 5, 7):
            b_copy(q).wait_send()

        @pl.when(c0)
        def _():
            dv = rcopy(
                R.gp.at[128:896, 0:1536], o_g.at[:, 0:1536], S.dv_s.at[0], S.dv_r.at[0], core_peer
            )
            dv.wait_recv()


def fused(counts, tokens, cotan, w_in, w_down, gain, bias, pos):
    hbm = pl.BlockSpec(memory_space=pl.ANY)
    vmem = pl.BlockSpec(memory_space=pltpu.VMEM)
    out = jax.ShapeDtypeStruct
    return pl.pallas_call(
        kernel,
        in_specs=[pl.BlockSpec(memory_space=pltpu.SMEM), hbm, hbm, hbm, hbm, vmem, vmem, vmem],
        out_specs=[hbm] * 6,
        out_shape=[
            out((512, D), bf16),
            out((16, D), f32),
            out((512, D), bf16),
            out((D, 4608), bf16),
            out((8, D), f32),
            out((8, 192), f32),
        ],
        scratch_shapes=[pltpu.VMEM(s, d) for s, d in SCRATCH.values()]
        + [pltpu.SemaphoreType.DMA((n,)) for n in SEMS.values()],
        compiler_params=pltpu.CompilerParams(
            collective_id=0, has_side_effects=True, vmem_limit_bytes=64 * 2**20 - 2**17
        ),
        name="layers",
    )(counts, tokens, cotan, w_in, w_down, gain, bias, pos)


def shards(tokens, seg_counts, w_in, w_down, ln_gain, ln_bias, pos_table, cotangent):
    sec = lax.axis_index("section")
    a1, a3, gt, g, gg, gpos = fused(
        seg_counts,
        tokens.reshape(512, D),
        cotangent.reshape(512, D),
        w_in[0],
        w_down,
        ln_gain,
        ln_bias,
        pos_table,
    )
    own = lax.dynamic_slice(seg_counts, (0, 2 * sec), (2, 2))
    top = lax.dynamic_slice(a3, (lax.rem(sec, 2) * 8 + lax.div(sec, 2) * 4, 0), (4, D))
    place = lax.broadcasted_iota(jnp.int32, (2, 2, 128, 1), 2)
    mixed = jnp.where(place == 0, top.reshape(2, 2, 1, D).astype(bf16), a1.reshape(2, 2, 128, D))
    mixed = jnp.where(place < own[:, :, None, None], mixed, jnp.zeros((), bf16))
    return (
        mixed.reshape(2, 256, D),
        gt.astype(f32).reshape(2, 256, D),
        g[:, 1536:].astype(f32)[None],
        g[:, :1536].astype(f32).T,
        gg[0:1],
        gg[1:2],
        gpos,
    )


def solution(mesh):
    return jax.shard_map(
        shards,
        mesh=mesh,
        in_specs=(
            P("dp", "section", None),
            P("dp", None),
            P("section", None, None),
            P("section", None),
            P("section", None),
            P("section", None),
            P(None, "section"),
            P("dp", "section", None),
        ),
        out_specs=(
            P("dp", "section", None),
            P("dp", "section", None),
            P("section", None, None),
            P("section", None),
            P("section", None),
            P("section", None),
            P(None, "section"),
        ),
        check_vma=False,
    )
```

time: 1900 us -> 281 us (0.15); the launches traced: 1870 us -> 280 us
  waiting for transfers between devices: 641 us -> 0 us
  matrix products: 422 us -> 0 us
  Pallas kernels: 0 us -> 255 us
  local copies, waits for them, and re-layouts: 245 us -> 9.05 us
  other arithmetic: 245 us -> 15.3 us
  starting transfers between devices: 160 us -> 0 us
  loops' own time: 98.4 us -> 0 us
  blocking collectives: 43 us -> 0 us
    psum x1 -> x0, waiting for transfers between devices: 565 us -> none  [shards(): lax.psum((grad_weight, grad_down, grad_gain, grad_bias, pos_part), 'dp')]
    dot_general x70 -> x0, matrix products: 349 us -> none  [the longest x10 60.6 us: attend(): jnp.einsum('nsd,de->nse', rows, weight[:, :3 * model_width], preferred_el...]
    pallas_call x0 -> x1, Pallas kernels: none -> 255 us  [fused(): pl.pallas_call(kernel, in_specs=[pl.BlockSpec(memory_space=pltpu.SMEM), h...]
    ppermute x12 -> x0, starting transfers between devices: 160 us -> none  [from_behind(): return lax.ppermute(block, axis, route)]
    another operation x12 -> x0, loops' own time: 98.4 us -> none  [the longest x5 85.5 us: backward_tick(): lax.switch(section_index, backward_parts, section_in, grad_in, counts)]
    slice x41 -> x1, local copies, waits for them, and re-layouts: 97.6 us -> 1.4 us  [shards(): gg[1:2]]
    add x20 -> x0, other arithmetic: 89.1 us -> none  [add_active(): return total + jnp.where(active, term, 0.0)]
    sub x10 -> x0, matrix products: 73.1 us -> none  [attend(): probability = jax.nn.softmax(scores, axis=-1)]
  transfers between devices with their start and end apart: 18 -> 0, of which waited for: 5 -> 0; matrix products, arithmetic and copies ran while one was open for 17% -> 0% of each run, Pallas kernels for 0% -> 0%
where the time goes in v1:
time: 281 us; the launch traced here: 280 us
  Pallas kernels  255 us (91%)
  other arithmetic  15.3 us (5%)
  local copies, waits for them, and re-layouts  9.05 us (3%)
    pallas_call x1, Pallas kernels, fused(): pl.pallas_call(kernel, in_specs=[pl.BlockSpec(memory_space=pltpu.SMEM), h...  255 us
    broadcast_in_dim x1, other arithmetic, shards(): g[:, 1536:].astype(f32)[None]  7.37 us
    unnamed x9, local copies, waits for them, and re-layouts  6.8 us

profile of v1, /device:TPU:0, one launch (start us, length us, event | category | flops | bytes accessed | tf_op | source)
XLA Modules:
  0.0 280.2 jit_solution(16525121659983589082)
XLA Ops:
  0.6 0.0 copy-start.2
  0.7 255.1 %layers.1 = (bf16[512,768]{1,0:T(8,128)(2,1)}, f32[16,768]{1,0:T(8,128)}, bf16[512,768]{1,0:T(8,128)(2,1)}, bf16[768,4608]{1,0:T(8,128)(2,1)}, f32[8,768]{1,0:T(8,128)}, /*index=5*/f32[8,192]{1,0:T(8,128)}) custom-call(s32[2,8]{1,0:T(2,128)} %counts.1, bf16[512,768]{1,0:T(8,128)(2,1)} %bitcast.24, bf16[512,768]{1,0:T(8,128)(2,1)} %bitcast.25, ...), custom_call_target="tpu_custom_call" | custom-call | tf_op jit(solution)/shard_map/layers/pallas_call | solution.py:1077
  255.8 0.8 dynamic-slice_convert_fusion
  256.5 0.0 copy-done.2
  256.5 0.1 constant_dynamic-slice_fusion
  256.6 0.1 broadcast_bitcast_fusion
  256.7 2.2 fusion
  258.9 7.4 %bitcast_convert_fusion = f32[1,768,3072]{2,1,0:T(8,128)} fusion(bf16[768,4608]{1,0:T(8,128)(2,1)} %get-tuple-element.16), kind=kLoop, calls=%fused_computation | loop fusion | flops 2359296 | bytes 14155776 | tf_op jit(solution)/shard_map/broadcast_in_dim | solution.py:1118
  266.3 4.5 %convert_bitcast_fusion = f32[1536,768]{0,1:T(8,128)} fusion(bf16[768,4608]{1,0:T(8,128)(2,1)} %get-tuple-element.16), kind=kLoop, calls=%fused_computation.1 | loop fusion | flops 1179648 | bytes 7077888 | tf_op jit(solution)/shard_map/transpose | solution.py:1119
  270.8 0.0 copy-start
  270.8 0.0 copy-start.1
  270.8 6.1 %copy.15 = f32[1536,768]{1,0:T(8,128)} copy(f32[1536,768]{0,1:T(8,128)} %convert_bitcast_fusion) | data formatting | bytes 9437184
  276.9 1.4 fusion.1
  278.3 0.0 copy-done
  278.3 1.3 convert.3
  279.6 0.0 copy-done.1
  279.6 0.6 copy.19
  (5 shorter events, 0.0 us)
Async XLA Ops:
  0.6 255.9 %copy-start.2 = (s32[2,8]{1,0:T(2,128)S(1)}, s32[2,8]{1,0:T(2,128)}, u32[]{:S(2)}) copy-start(s32[2,8]{1,0:T(2,128)} %counts.1) | copy-start | bytes 196
  270.8 7.5 %copy-start = (bf16[512,768]{1,0:T(8,128)(2,1)S(1)}, bf16[512,768]{1,0:T(8,128)(2,1)}, u32[]{:S(2)}) copy-start(bf16[512,768]{1,0:T(8,128)(2,1)} %get-tuple-element.15) | copy-start | bytes 2359300
  270.8 8.8 %copy-start.1 = (f32[8,192]{1,0:T(8,128)S(1)}, f32[8,192]{1,0:T(8,128)}, u32[]{:S(2)}) copy-start(f32[8,192]{1,0:T(8,128)} %get-tuple-element.41) | copy-start | bytes 18436
